TPU v7x, 512 devices: a whole 4x4x16 slice. The times are simulated.
512 devices in a mesh: outer: 32 (over y, z_lo), inner: 16 (over z_hi, x, core).
Axes of the slice: x: 4, y: 4, z: 16 (z_hi: 2, z_lo: 8; z = z_hi * 8 + z_lo), core: 2. Of those that a mesh axis runs over, the one named last changes fastest.
Arguments:
- image_embed: bfloat16 [131072, 768], P(('outer', 'inner')), may hold values from -1 to 1
- text_embed: bfloat16 [131072, 768], P(('outer', 'inner')), may hold values from -1 to 1
- positive: int32 [512, 256], P(('outer', 'inner')), may hold values from 0 to 255, each once within a row
- row_weight: bfloat16 [131072], P(('outer', 'inner')), may hold values from 0.5 to 18
- logit_scale: float32 [1], replicated, may hold values from 10 to 30
Outputs:
- loss: float32 [1], replicated
- scale_grad: float32 [1], replicated
- image_grad: bfloat16 [131072, 768], P(('outer', 'inner'))
- text_grad: bfloat16 [131072, 768], P(('outer', 'inner'))
Inputs may be any that keep to these rules, and one draw needn't show every extreme that they name: `positive`: each row of 256 entries names every text row of its block once.
All inputs are finite; a program needn't handle non-finite values.
Results may differ from a plain program's by a relative error of at most 0.0049.
Values may be sent and summed in bfloat16 or wider, within the bound.
A program may use at most 64 MiB of HBM per device.

v0:
```python
from functools import reduce

import jax
import jax.numpy as jnp
from jax import lax
from jax.sharding import PartitionSpec as P


def passed_along(block, axis, distance):
    devices = range(lax.axis_size(axis))
    route = [((i - distance) % len(devices), i) for i in devices]
    return lax.ppermute(block, axis, route)


def pair_logits(left, right, temper):
    return temper * jnp.einsum("rd,cd->rc", left, right, preferred_element_type=jnp.float32)


def coefficient(logits, row_lse, col_lse, row_w, col_w, diag_mark, factor):
    result_tile = factor * (
        row_w[:, None] * (jnp.exp(logits - row_lse[:, None]) - diag_mark)
        + col_w[None, :] * (jnp.exp(logits - col_lse[None, :]) - diag_mark)
    )
    return result_tile.astype(jnp.bfloat16)


def ahead_texts(text_embed, row_weight, cycle_steps):
    blocks = [(text_embed, row_weight)]
    current = (text_embed, row_weight)
    for offset in range(cycle_steps):
        current = passed_along((current[0], current[1]), "inner", -1)
        blocks.append(current)
    return blocks


def ahead_lse(col_lse, cycle_steps):
    blocks = [col_lse]
    current = col_lse
    for offset in range(cycle_steps):
        current = passed_along(current, "inner", -1)
        blocks.append(current)
    return blocks


def home_merge(partials, cycle_steps):
    running = partials[cycle_steps]
    for offset in range(cycle_steps):
        arrived = passed_along(running, "inner", 1)
        running = jnp.logaddexp(arrived, partials[cycle_steps - 1 - offset])
    return running


def home_sum(partials, cycle_steps):
    running = partials[cycle_steps]
    for offset in range(cycle_steps):
        arrived = passed_along(running, "inner", 1)
        running = arrived + partials[cycle_steps - 1 - offset]
    return running


def per_device(image_embed, text_embed, positive, row_weight, logit_scale):
    row_count, width = image_embed.shape
    cycle_steps = min(4, lax.axis_size("inner") - 1)
    pairs = row_count * lax.axis_size("outer") * lax.axis_size("inner")
    temper = logit_scale[0]
    own_weight = row_weight.astype(jnp.float32)
    total_weight = lax.psum(jnp.sum(own_weight), ("outer", "inner"))
    factor = pairs / (2.0 * total_weight)
    marker = (
        lax.broadcasted_iota(jnp.int32, (row_count, row_count), 1) == positive[0][:, None]
    ).astype(jnp.float32)
    text_blocks = ahead_texts(text_embed, row_weight, cycle_steps)
    tile_list = [pair_logits(image_embed, entry[0], temper) for entry in text_blocks]
    row_max = reduce(jnp.maximum, [jnp.max(logit_tile, axis=1) for logit_tile in tile_list])
    row_lse = row_max + jnp.log(
        sum((jnp.sum(jnp.exp(logit_tile - row_max[:, None]), axis=1) for logit_tile in tile_list))
    )
    col_lse = home_merge(
        [jax.nn.logsumexp(logit_tile, axis=0) for logit_tile in tile_list], cycle_steps
    )
    col_blocks = ahead_lse(col_lse, cycle_steps)
    image_sum = jnp.zeros((row_count, width), jnp.float32)
    partials = []
    for offset in range(cycle_steps + 1):
        diag_mark = marker if offset == 0 else 0.0
        coef_tile = coefficient(
            tile_list[offset],
            row_lse,
            col_blocks[offset],
            own_weight,
            text_blocks[offset][1].astype(jnp.float32),
            diag_mark,
            factor,
        )
        image_sum = image_sum + jnp.dot(
            coef_tile, text_blocks[offset][0], preferred_element_type=jnp.float32
        )
        partials.append(
            jnp.einsum("rc,rd->cd", coef_tile, image_embed, preferred_element_type=jnp.float32)
        )
    text_sum = home_sum(partials, cycle_steps)
    positive_logit = jnp.sum(tile_list[0] * marker, axis=1)
    column_logit = jnp.sum(tile_list[0] * marker, axis=0)
    loss_part = jnp.sum(own_weight * (row_lse - positive_logit)) + jnp.sum(
        own_weight * (col_lse - column_logit)
    )
    scale_part = jnp.sum(image_embed.astype(jnp.float32) * image_sum)
    loss_total, scale_total = lax.psum((loss_part, scale_part), ("outer", "inner"))
    loss = jnp.reshape(loss_total / (2.0 * total_weight), (1,))
    scale_grad = jnp.reshape(scale_total / pairs, (1,))
    return (
        loss,
        scale_grad,
        (temper * image_sum).astype(jnp.bfloat16),
        (temper * text_sum).astype(jnp.bfloat16),
    )


def solution(mesh):
    in_specs = (
        P(("outer", "inner"), None),
        P(("outer", "inner"), None),
        P(("outer", "inner"), None),
        P(("outer", "inner")),
        P(),
    )
    out_specs = (P(), P(), P(("outer", "inner"), None), P(("outer", "inner"), None))
    return jax.shard_map(
        per_device, mesh=mesh, in_specs=in_specs, out_specs=out_specs, check_vma=False
    )
```

profile of v0, /device:TPU:1, one launch (start us, length us, event | category | flops | bytes accessed | tf_op | source)
XLA Modules:
  0.0 608.8 jit_solution(2374243904389351082)
XLA Ops:
  0.6 8.8 %collective-permute-start = (bf16[256,768]{1,0:T(8,128)(2,1)}, bf16[256,768]{1,0:T(8,128)(2,1)S(1)}, u32[]{:S(2)}, u32[]{:S(2)}) collective-permute-start(bf16[256,768]{1,0:T(8,128)(2,1)} %param.6), channel_id=1, source_target_pairs={{1,0},{2,1},{3,2},{4,3},{5,4},{6,5},{7,6},{8,7},{9,8},{10,9},{11,1... | collective-permute-start | bytes 1179656 | tf_op jit(solution)/shard_map/ppermute | solution.py:12
  11.7 27.1 %collective-permute-start.1 = (bf16[256,768]{1,0:T(8,128)(2,1)S(1)}, bf16[256,768]{1,0:T(8,128)(2,1)S(1)}, u32[]{:S(2)}, u32[]{:S(2)}) collective-permute-start(bf16[256,768]{1,0:T(8,128)(2,1)S(1)} %collective-permute-done), channel_id=1, source_target_pairs={{1,0},{2,1},{3,2},{4,3},{5,4},{6,5},{7,6},{8,7},{9,8},{10,9},{11,1... | collective-permute-start | bytes 1179656 | tf_op jit(solution)/shard_map/ppermute | solution.py:12
  40.1 24.4 %collective-permute-start.2 = (bf16[256,768]{1,0:T(8,128)(2,1)S(1)}, bf16[256,768]{1,0:T(8,128)(2,1)S(1)}, u32[]{:S(2)}, u32[]{:S(2)}) collective-permute-start(bf16[256,768]{1,0:T(8,128)(2,1)S(1)} %collective-permute-done.1), channel_id=1, source_target_pairs={{1,0},{2,1},{3,2},{4,3},{5,4},{6,5},{7,6},{8,7},{9,8},{10,9},{11,1... | collective-permute-start | bytes 1179656 | tf_op jit(solution)/shard_map/ppermute | solution.py:12
  65.9 21.8 %collective-permute-start.3 = (bf16[256,768]{1,0:T(8,128)(2,1)S(1)}, bf16[256,768]{1,0:T(8,128)(2,1)S(1)}, u32[]{:S(2)}, u32[]{:S(2)}) collective-permute-start(bf16[256,768]{1,0:T(8,128)(2,1)S(1)} %collective-permute-done.2), channel_id=1, source_target_pairs={{1,0},{2,1},{3,2},{4,3},{5,4},{6,5},{7,6},{8,7},{9,8},{10,9},{11,1... | collective-permute-start | bytes 1179656 | tf_op jit(solution)/shard_map/ppermute | solution.py:12
  93.0 17.5 %collective-permute-done.4 = f32[256]{0:T(256)S(1)} collective-permute-done((f32[256]{0:T(256)S(1)}, f32[256]{0:T(256)S(1)}, u32[]{:S(2)}, u32[]{:S(2)}) %collective-permute-start.4) | collective-permute-done | bytes 1056 | tf_op jit(solution)/shard_map/ppermute | solution.py:12
  110.5 1.9 collective-permute-start.5
  112.4 14.0 %collective-permute-done.5 = f32[256]{0:T(256)S(1)} collective-permute-done((f32[256]{0:T(256)S(1)}, f32[256]{0:T(256)S(1)}, u32[]{:S(2)}, u32[]{:S(2)}) %collective-permute-start.5) | collective-permute-done | bytes 1056 | tf_op jit(solution)/shard_map/ppermute | solution.py:12
  128.4 13.8 %collective-permute-done.6 = f32[256]{0:T(256)S(1)} collective-permute-done((f32[256]{0:T(256)S(1)}, f32[256]{0:T(256)S(1)}, u32[]{:S(2)}, u32[]{:S(2)}) %collective-permute-start.6) | collective-permute-done | bytes 1056 | tf_op jit(solution)/shard_map/ppermute | solution.py:12
  144.1 13.8 %collective-permute-done.7 = f32[256]{0:T(256)S(1)} collective-permute-done((f32[256]{0:T(256)S(1)}, f32[256]{0:T(256)S(1)}, u32[]{:S(2)}, u32[]{:S(2)}) %collective-permute-start.7) | collective-permute-done | bytes 1056 | tf_op jit(solution)/shard_map/ppermute | solution.py:12
  159.2 15.1 %collective-permute-start.9 = (f32[256]{0:T(256)S(1)}, f32[256]{0:T(256)S(1)}, u32[]{:S(2)}, u32[]{:S(2)}) collective-permute-start(f32[256]{0:T(256)S(1)} %get-tuple-element.31), channel_id=1, source_target_pairs={{1,0},{2,1},{3,2},{4,3},{5,4},{6,5},{7,6},{8,7},{9,8},{10,9},{11,1... | collective-permute-start | bytes 3080 | tf_op jit(solution)/shard_map/ppermute | solution.py:12
  175.1 2.4 collective-permute-start.11
  177.5 14.4 %collective-permute-start.8 = (bf16[256]{0:T(256)(128)(2,1)S(1)}, bf16[256]{0:T(256)(128)(2,1)S(1)}, u32[]{:S(2)}, u32[]{:S(2)}) collective-permute-start(bf16[256]{0:T(256)(128)(2,1)S(1)} %copy-done.7), channel_id=1, source_target_pairs={{1,0},{2,1},{3,2},{4,3},{5,4},{6,5},{7,6},{8,7},{9,8},{10,9},{11,1... | collective-permute-start | bytes 1544 | tf_op jit(solution)/shard_map/ppermute | solution.py:12
  193.9 13.8 %collective-permute-start.10 = (bf16[256]{0:T(256)(128)(2,1)S(1)}, bf16[256]{0:T(256)(128)(2,1)S(1)}, u32[]{:S(2)}, u32[]{:S(2)}) collective-permute-start(bf16[256]{0:T(256)(128)(2,1)S(1)} %collective-permute-done.8), channel_id=1, source_target_pairs={{1,0},{2,1},{3,2},{4,3},{5,4},{6,5},{7,6},{8,7},{9,8},{10,9},{11,1... | collective-permute-start | bytes 1544 | tf_op jit(solution)/shard_map/ppermute | solution.py:12
  208.4 2.4 collective-permute-start.12
  210.8 14.4 %collective-permute-start.15 = (f32[256]{0:T(256)S(1)}, f32[256]{0:T(256)S(1)}, u32[]{:S(2)}, u32[]{:S(2)}) collective-permute-start(f32[256]{0:T(256)S(1)} %collective-permute-done.13), channel_id=1, source_target_pairs={{1,0},{2,1},{3,2},{4,3},{5,4},{6,5},{7,6},{8,7},{9,8},{10,9},{11,1... | collective-permute-start | bytes 3080 | tf_op jit(solution)/shard_map/ppermute | solution.py:12
  227.2 2.9 collective-permute-done.14
  230.1 127.1 %psum.22 = f32[]{:T(128)} all-reduce(f32[]{:T(128)} %get-tuple-element.26), channel_id=1, replica_groups=mesh['outer'=32,'inner'=16] {'outer','inner'}, use_global_device_ids=true, to_apply=%region_26.0 | all-reduce | flops 1 | bytes 8 | tf_op jit(solution)/shard_map/psum | solution.py:67
  360.3 8.9 %collective-permute-done.16 = f32[256,768]{1,0:T(8,128)S(1)} collective-permute-done((f32[256,768]{1,0:T(8,128)S(1)}, f32[256,768]{1,0:T(8,128)S(1)}, u32[]{:S(2)}, u32[]{:S(2)}) %collective-permute-start.16) | collective-permute-done | bytes 786464 | tf_op jit(solution)/shard_map/ppermute | solution.py:12
  370.5 4.4 collective-permute-start.17
  376.6 37.6 %collective-permute-done.17 = f32[256,768]{1,0:T(8,128)} collective-permute-done((f32[256,768]{1,0:T(8,128)}, f32[256,768]{1,0:T(8,128)}, u32[]{:S(2)}, u32[]{:S(2)}) %collective-permute-start.17) | collective-permute-done | bytes 786464 | tf_op jit(solution)/shard_map/ppermute | solution.py:12
  418.9 37.4 %collective-permute-done.18 = f32[256,768]{1,0:T(8,128)S(1)} collective-permute-done((f32[256,768]{1,0:T(8,128)S(1)}, f32[256,768]{1,0:T(8,128)S(1)}, u32[]{:S(2)}, u32[]{:S(2)}) %collective-permute-start.18) | collective-permute-done | bytes 786464 | tf_op jit(solution)/shard_map/ppermute | solution.py:12
  457.3 2.0 collective-permute-start.19
  462.4 140.9 %all-reduce = (f32[]{:T(128)}, f32[]{:T(128)}) all-reduce(f32[]{:T(128)S(6)} %add.140, f32[]{:T(128)} %get-tuple-element.34), channel_id=1, replica_groups=mesh['outer'=32,'inner'=16] {'outer','inner'}, use_global_device_ids=true, to_apply=%region_24.0 | all-reduce | flops 2 | bytes 16 | tf_op jit(solution)/shard_map/psum | solution.py:108
  604.6 2.0 multiply_convert_fusion
  (67 shorter events, 32.8 us)
Async XLA Ops:
  0.6 11.0 %collective-permute-start = (bf16[256,768]{1,0:T(8,128)(2,1)}, bf16[256,768]{1,0:T(8,128)(2,1)S(1)}, u32[]{:S(2)}, u32[]{:S(2)}) collective-permute-start(bf16[256,768]{1,0:T(8,128)(2,1)} %param.6), channel_id=1, source_target_pairs={{1,0},{2,1},{3,2},{4,3},{5,4},{6,5},{7,6},{8,7},{9,8},{10,9},{11,1... | collective-permute-start | bytes 1179656 | tf_op jit(solution)/shard_map/ppermute | solution.py:12
  10.1 28.7 %copy-start = (bf16[256,768]{1,0:T(8,128)(2,1)S(1)}, bf16[256,768]{1,0:T(8,128)(2,1)}, u32[]{:S(2)}) copy-start(bf16[256,768]{1,0:T(8,128)(2,1)} %param.5) | copy-start | bytes 1179652
  11.7 28.5 %collective-permute-start.1 = (bf16[256,768]{1,0:T(8,128)(2,1)S(1)}, bf16[256,768]{1,0:T(8,128)(2,1)S(1)}, u32[]{:S(2)}, u32[]{:S(2)}) collective-permute-start(bf16[256,768]{1,0:T(8,128)(2,1)S(1)} %collective-permute-done), channel_id=1, source_target_pairs={{1,0},{2,1},{3,2},{4,3},{5,4},{6,5},{7,6},{8,7},{9,8},{10,9},{11,1... | collective-permute-start | bytes 1179656 | tf_op jit(solution)/shard_map/ppermute | solution.py:12
  40.1 25.7 %collective-permute-start.2 = (bf16[256,768]{1,0:T(8,128)(2,1)S(1)}, bf16[256,768]{1,0:T(8,128)(2,1)S(1)}, u32[]{:S(2)}, u32[]{:S(2)}) collective-permute-start(bf16[256,768]{1,0:T(8,128)(2,1)S(1)} %collective-permute-done.1), channel_id=1, source_target_pairs={{1,0},{2,1},{3,2},{4,3},{5,4},{6,5},{7,6},{8,7},{9,8},{10,9},{11,1... | collective-permute-start | bytes 1179656 | tf_op jit(solution)/shard_map/ppermute | solution.py:12
  65.9 22.2 %copy-start.1 = (bf16[256,768]{1,0:T(8,128)(2,1)}, bf16[256,768]{1,0:T(8,128)(2,1)S(1)}, u32[]{:S(2)}) copy-start(bf16[256,768]{1,0:T(8,128)(2,1)S(1)} %collective-permute-done.2) | copy-start | bytes 1179652
  65.9 23.1 %collective-permute-start.3 = (bf16[256,768]{1,0:T(8,128)(2,1)S(1)}, bf16[256,768]{1,0:T(8,128)(2,1)S(1)}, u32[]{:S(2)}, u32[]{:S(2)}) collective-permute-start(bf16[256,768]{1,0:T(8,128)(2,1)S(1)} %collective-permute-done.2), channel_id=1, source_target_pairs={{1,0},{2,1},{3,2},{4,3},{5,4},{6,5},{7,6},{8,7},{9,8},{10,9},{11,1... | collective-permute-start | bytes 1179656 | tf_op jit(solution)/shard_map/ppermute | solution.py:12
  91.0 19.5 %collective-permute-start.4 = (f32[256]{0:T(256)S(1)}, f32[256]{0:T(256)S(1)}, u32[]{:S(2)}, u32[]{:S(2)}) collective-permute-start(f32[256]{0:T(256)S(1)} %log_add_fusion), channel_id=1, source_target_pairs={{15,0},{0,1},{1,2},{2,3},{3,4},{4,5},{5,6},{6,7},{7,8},{8,9},{9,10... | collective-permute-start | bytes 3080 | tf_op jit(solution)/shard_map/ppermute | solution.py:12
  110.5 15.9 %collective-permute-start.5 = (f32[256]{0:T(256)S(1)}, f32[256]{0:T(256)S(1)}, u32[]{:S(2)}, u32[]{:S(2)}) collective-permute-start(f32[256]{0:T(256)S(1)} %compare_select_fusion.3), channel_id=1, source_target_pairs={{15,0},{0,1},{1,2},{2,3},{3,4},{4,5},{5,6},{6,7},{7,8},{8,9},{9,10... | collective-permute-start | bytes 3080 | tf_op jit(solution)/shard_map/ppermute | solution.py:12
  126.4 15.7 %collective-permute-start.6 = (f32[256]{0:T(256)S(1)}, f32[256]{0:T(256)S(1)}, u32[]{:S(2)}, u32[]{:S(2)}) collective-permute-start(f32[256]{0:T(256)S(1)} %compare_select_fusion.2), channel_id=1, source_target_pairs={{15,0},{0,1},{1,2},{2,3},{3,4},{4,5},{5,6},{6,7},{7,8},{8,9},{9,10... | collective-permute-start | bytes 3080 | tf_op jit(solution)/shard_map/ppermute | solution.py:12
  142.2 15.7 %collective-permute-start.7 = (f32[256]{0:T(256)S(1)}, f32[256]{0:T(256)S(1)}, u32[]{:S(2)}, u32[]{:S(2)}) collective-permute-start(f32[256]{0:T(256)S(1)} %compare_select_fusion.1), channel_id=1, source_target_pairs={{15,0},{0,1},{1,2},{2,3},{3,4},{4,5},{5,6},{6,7},{7,8},{8,9},{9,10... | collective-permute-start | bytes 3080 | tf_op jit(solution)/shard_map/ppermute | solution.py:12
  159.2 15.9 %collective-permute-start.9 = (f32[256]{0:T(256)S(1)}, f32[256]{0:T(256)S(1)}, u32[]{:S(2)}, u32[]{:S(2)}) collective-permute-start(f32[256]{0:T(256)S(1)} %get-tuple-element.31), channel_id=1, source_target_pairs={{1,0},{2,1},{3,2},{4,3},{5,4},{6,5},{7,6},{8,7},{9,8},{10,9},{11,1... | collective-permute-start | bytes 3080 | tf_op jit(solution)/shard_map/ppermute | solution.py:12
  175.1 16.8 %collective-permute-start.11 = (f32[256]{0:T(256)S(1)}, f32[256]{0:T(256)S(1)}, u32[]{:S(2)}, u32[]{:S(2)}) collective-permute-start(f32[256]{0:T(256)S(1)} %collective-permute-done.9), channel_id=1, source_target_pairs={{1,0},{2,1},{3,2},{4,3},{5,4},{6,5},{7,6},{8,7},{9,8},{10,9},{11,1... | collective-permute-start | bytes 3080 | tf_op jit(solution)/shard_map/ppermute | solution.py:12
  177.5 16.4 %collective-permute-start.8 = (bf16[256]{0:T(256)(128)(2,1)S(1)}, bf16[256]{0:T(256)(128)(2,1)S(1)}, u32[]{:S(2)}, u32[]{:S(2)}) collective-permute-start(bf16[256]{0:T(256)(128)(2,1)S(1)} %copy-done.7), channel_id=1, source_target_pairs={{1,0},{2,1},{3,2},{4,3},{5,4},{6,5},{7,6},{8,7},{9,8},{10,9},{11,1... | collective-permute-start | bytes 1544 | tf_op jit(solution)/shard_map/ppermute | solution.py:12
  191.9 18.9 %collective-permute-start.13 = (f32[256]{0:T(256)S(1)}, f32[256]{0:T(256)S(1)}, u32[]{:S(2)}, u32[]{:S(2)}) collective-permute-start(f32[256]{0:T(256)S(1)} %collective-permute-done.11), channel_id=1, source_target_pairs={{1,0},{2,1},{3,2},{4,3},{5,4},{6,5},{7,6},{8,7},{9,8},{10,9},{11,1... | collective-permute-start | bytes 3080 | tf_op jit(solution)/shard_map/ppermute | solution.py:12
  193.9 14.6 %collective-permute-start.10 = (bf16[256]{0:T(256)(128)(2,1)S(1)}, bf16[256]{0:T(256)(128)(2,1)S(1)}, u32[]{:S(2)}, u32[]{:S(2)}) collective-permute-start(bf16[256]{0:T(256)(128)(2,1)S(1)} %collective-permute-done.8), channel_id=1, source_target_pairs={{1,0},{2,1},{3,2},{4,3},{5,4},{6,5},{7,6},{8,7},{9,8},{10,9},{11,1... | collective-permute-start | bytes 1544 | tf_op jit(solution)/shard_map/ppermute | solution.py:12
  208.4 16.8 %collective-permute-start.12 = (bf16[256]{0:T(256)(128)(2,1)S(1)}, bf16[256]{0:T(256)(128)(2,1)S(1)}, u32[]{:S(2)}, u32[]{:S(2)}) collective-permute-start(bf16[256]{0:T(256)(128)(2,1)S(1)} %collective-permute-done.10), channel_id=1, source_target_pairs={{1,0},{2,1},{3,2},{4,3},{5,4},{6,5},{7,6},{8,7},{9,8},{10,9},{11,1... | collective-permute-start | bytes 1544 | tf_op jit(solution)/shard_map/ppermute | solution.py:12
  210.8 147.1 %collective-permute-start.15 = (f32[256]{0:T(256)S(1)}, f32[256]{0:T(256)S(1)}, u32[]{:S(2)}, u32[]{:S(2)}) collective-permute-start(f32[256]{0:T(256)S(1)} %collective-permute-done.13), channel_id=1, source_target_pairs={{1,0},{2,1},{3,2},{4,3},{5,4},{6,5},{7,6},{8,7},{9,8},{10,9},{11,1... | collective-permute-start | bytes 3080 | tf_op jit(solution)/shard_map/ppermute | solution.py:12
  225.3 4.9 collective-permute-start.14
  358.4 10.8 %collective-permute-start.16 = (f32[256,768]{1,0:T(8,128)S(1)}, f32[256,768]{1,0:T(8,128)S(1)}, u32[]{:S(2)}, u32[]{:S(2)}) collective-permute-start(f32[256,768]{1,0:T(8,128)S(1)} %fusion.11), channel_id=1, source_target_pairs={{15,0},{0,1},{1,2},{2,3},{3,4},{4,5},{5,6},{6,7},{7,8},{8,9},{9,10... | collective-permute-start | bytes 2359304 | tf_op jit(solution)/shard_map/ppermute | solution.py:12
  360.3 15.9 %copy-start.5 = (bf16[256,768]{1,0:T(8,128)(2,1)S(1)}, bf16[256,768]{1,0:T(8,128)(2,1)}, u32[]{:S(2)}) copy-start(bf16[256,768]{1,0:T(8,128)(2,1)} %param.6) | copy-start | bytes 1179652
  370.5 43.6 %collective-permute-start.17 = (f32[256,768]{1,0:T(8,128)}, f32[256,768]{1,0:T(8,128)}, u32[]{:S(2)}, u32[]{:S(2)}) collective-permute-start(f32[256,768]{1,0:T(8,128)} %convolution_add_fusion), channel_id=1, source_target_pairs={{15,0},{0,1},{1,2},{2,3},{3,4},{4,5},{5,6},{6,7},{7,8},{8,9},{9,10... | collective-permute-start | bytes 2359304 | tf_op jit(solution)/shard_map/ppermute | solution.py:12
  415.7 40.6 %collective-permute-start.18 = (f32[256,768]{1,0:T(8,128)S(1)}, f32[256,768]{1,0:T(8,128)S(1)}, u32[]{:S(2)}, u32[]{:S(2)}) collective-permute-start(f32[256,768]{1,0:T(8,128)S(1)} %fusion.10), channel_id=1, source_target_pairs={{15,0},{0,1},{1,2},{2,3},{3,4},{4,5},{5,6},{6,7},{7,8},{8,9},{9,10... | collective-permute-start | bytes 2359304 | tf_op jit(solution)/shard_map/ppermute | solution.py:12
  457.3 2.4 copy-start.2
  457.3 147.3 %collective-permute-start.19 = (f32[256,768]{1,0:T(8,128)}, f32[256,768]{1,0:T(8,128)}, u32[]{:S(2)}, u32[]{:S(2)}) collective-permute-start(f32[256,768]{1,0:T(8,128)} %add.152), channel_id=1, source_target_pairs={{15,0},{0,1},{1,2},{2,3},{3,4},{4,5},{5,6},{6,7},{7,8},{8,9},{9,10... | collective-permute-start | bytes 2359304 | tf_op jit(solution)/shard_map/ppermute | solution.py:12
  (4 other events, 3.1 us)
where the time goes:
time: 610 us; the launch traced here: 609 us
  blocking collectives  268 us (44%)
  starting transfers between devices  166 us (27%)
  waiting for transfers between devices  150 us (25%)
  matrix products  10.3 us (2%)
  between operations  7.25 us (1%)
    ppermute x20, starting transfers between devices, passed_along(): return lax.ppermute(block, axis, route)  166 us
    ppermute x20, waiting for transfers between devices, passed_along(): return lax.ppermute(block, axis, route)  150 us
    psum x1, blocking collectives, per_device(): lax.psum((loss_part, scale_part), ('outer', 'inner'))  141 us
    psum x1, blocking collectives, per_device(): total_weight = lax.psum(jnp.sum(own_weight), ('outer', 'inner'))  127 us
  transfers between devices with their start and end apart: 20, of which 13 were waited for; matrix products, arithmetic and copies ran while one was open for 1% of the time, Pallas kernels for 0%

commit v1 on v0

v1 whole, which is shorter than its diff:
```python
import functools

import jax
import jax.numpy as jnp
from jax import lax
from jax.experimental import pallas as pl
from jax.experimental.pallas import tpu as pltpu
from jax.sharding import PartitionSpec as P

MESH = pl.DeviceIdType.MESH
CHUNKS = 8
REACH = 4
X_SLOT, RELAY = 10, 11
(K_Z, K_XT, K_XI, K_HT, K_HI, K_HX, K_HR, K_C1, K_C2, K_C3, K_C4) = range(11)
LOW = -1e30
F32 = jnp.float32


def loop(low, high, body):
    def step(k, carry):
        body(k)
        return carry

    lax.fori_loop(low, high, step, 0)


def dot_nt(a, b):
    return lax.dot_general(a, b, (((1,), (1,)), ((), ())), preferred_element_type=F32)


def spread(row):
    return jnp.transpose(jnp.broadcast_to(row, (128, row.shape[1])))


def as_row(col):
    return jnp.transpose(col)[0:1]


def kernel(
    rows, n_z, img_ref, txt_ref, pos_ref, w_ref, scale_ref,
    ig_ref, tg_ref, loss_ref, sg_ref,
    blocks, logits, coefs, stat, diag, wcol, ls, rp, early_out, early_z, early, wp, wy, wz, ay, az,
    local_sem, send, recv, ls_s, ls_r, rp_s, rp_r, ez_s, ez_r, ef_s, ef_r, p_s, p_r, y_s, y_r, z_s, z_r,
):
    part = rows // CHUNKS
    outer, inner = lax.axis_index("outer"), lax.axis_index("inner")
    z_low = n_z // 2
    y, z = outer // z_low, (inner // 8) * z_low + outer % z_low
    p = inner % 8
    even = p % 2 == 0
    mate = p + 1 - 2 * (p % 2)
    half = p // 4
    q = p % 4

    def at(p_, z_, y_=None):
        y_ = y if y_ is None else (y_ + 4) % 4
        z_ = (z_ + n_z) % n_z
        return (y_ * z_low + z_ % z_low, (z_ // z_low) * 8 + (p_ + 8) % 8)

    far = at(p, z + z_low)

    def copy(src, dst, s_sem, r_sem, dev):
        return pltpu.make_async_remote_copy(
            src_ref=src, dst_ref=dst, send_sem=s_sem, recv_sem=r_sem, device_id=dev, device_id_type=MESH
        )

    text_in = pltpu.make_async_copy(txt_ref, blocks.at[0], local_sem.at[0])
    image_in = pltpu.make_async_copy(img_ref, blocks.at[5], local_sem.at[1])
    text_in.start()
    image_in.start()
    barrier = pltpu.get_barrier_semaphore()

    def hello(dev):
        pl.semaphore_signal(barrier, inc=1, device_id=dev, device_id_type=MESH)

    loop(1, 8, lambda d: hello(at(p + d, z)))
    loop(1, 4, lambda d: hello(at(p, z, y + d)))
    loop(1, n_z, lambda d: hello(at(p, z + d)))
    pl.semaphore_wait(barrier, 7 + 3 + n_z - 1)
    text_in.wait()
    image_in.wait()

    def chunk_copy(src, dst, k, dev, kind):
        r = pl.ds(pl.multiple_of(k * part, part), part)
        return copy(blocks.at[src, r], blocks.at[dst, r], send.at[kind, k], recv.at[dst, k], dev)

    def arrived(slot, k):
        chunk_copy(slot, slot, k, far, 0).wait_recv()

    crossing = jnp.where(half == 0, 0, 5)
    loop(0, CHUNKS, lambda k: chunk_copy(crossing, X_SLOT, k, far, K_Z).start())

    def send_own(k):
        pl.when(p >= 2)(lambda: chunk_copy(0, 2, k, at(p - 2, z), K_XT).start())
        pl.when(p <= 5)(lambda: chunk_copy(5, 7, k, at(p + 2, z), K_XI).start())
        pl.when(even)(lambda: chunk_copy(5, 6, k, at(mate, z), K_C1).start())
        pl.when(~even)(lambda: chunk_copy(0, 1, k, at(mate, z), K_C1).start())

    loop(0, CHUNKS, send_own)

    weight = w_ref[...]
    wcol[0] = spread(weight)
    wcol[1] = spread(jnp.log(weight))
    wp[p] = jnp.broadcast_to(jnp.sum(weight, axis=1, keepdims=True), (1, 128))
    loop(1, 8, lambda d: copy(wp.at[p], wp.at[p], p_s.at[d], p_r.at[d], at(p + d, z)).start())

    place = pos_ref[...]
    lanes = lax.broadcasted_iota(jnp.int32, (rows, rows), 1)
    subs = lax.broadcasted_iota(jnp.int32, (rows, rows), 0)
    place_col = spread(place.astype(F32)).astype(jnp.int32)[:, 0:1]
    wc = wcol[0]
    w_sub = jnp.concatenate([wc, wc], axis=1)
    diag[0] = jnp.where(lanes == place_col, w_sub + weight, 0.0)
    diag[1] = jnp.where(subs == place, w_sub + weight, 0.0)
    stat[:, 0] = jnp.full((2, rows, 128), LOW, F32)
    stat[:, 1:3] = jnp.zeros((2, 2, rows, 128), F32)
    rp[q] = jnp.full((4, rows), LOW, F32)
    temper = scale_ref[0]

    def tile(side, k):
        own = jnp.where(side == 0, 5, 0)
        other = jnp.where(side == 0, 0, 5) + k
        t = temper * dot_nt(blocks[own], blocks[other])
        logits[side, k] = t
        old = stat[side, 0]
        new = jnp.maximum(old, jnp.max(t, axis=1, keepdims=True))
        keep = jnp.exp(old - new)
        t0, t1 = t[:, :128], t[:, 128:]
        e0, e1 = jnp.exp(t0 - new), jnp.exp(t1 - new)
        stat[side, 0] = new
        stat[side, 1] = stat[side, 1] * keep + (e0 + e1)
        stat[side, 2] = stat[side, 2] * keep + (e0 * t0 + e1 * t1)

    def lse_of(side):
        total = jnp.broadcast_to(jnp.sum(stat[side, 1], axis=1, keepdims=True), (rows, 128))
        return stat[side, 0] + jnp.log(total)

    def hand_2(k, text, image):
        @pl.when(text)
        def _():
            arrived(2, k)
            pl.when(p >= 2)(lambda: chunk_copy(2, 4, k, at(p - 2, z), K_HT).start())
            chunk_copy(2, jnp.where(even, 1, 3), k, at(mate, z), K_C2).start()

        @pl.when(image)
        def _():
            arrived(7, k)
            pl.when(p <= 5)(lambda: chunk_copy(7, 9, k, at(p + 2, z), K_HI).start())
            chunk_copy(7, jnp.where(even, 8, 6), k, at(mate, z), K_C4).start()

    def hand_4(k, text, image):
        @pl.when(text)
        def _():
            arrived(4, k)
            pl.when(even)(lambda: chunk_copy(4, 3, k, at(mate, z), K_C3).start())

        @pl.when(image)
        def _():
            arrived(9, k)
            pl.when(~even)(lambda: chunk_copy(9, 8, k, at(mate, z), K_C3).start())

    loop(0, CHUNKS, lambda k: hand_2(k, p < 6, p > 1))

    def from_plane(d):
        o = (p + d) % 8
        copy(wp.at[o], wp.at[o], p_s.at[8 - d], p_r.at[8 - d], far).wait_recv()

    loop(1, 8, from_plane)
    wy[y] = jnp.sum(wp[...], axis=0)
    loop(1, 4, lambda d: copy(wy.at[y], wy.at[y], y_s.at[0, d], y_r.at[0, d], at(p, z, y + d)).start())

    loop(0, CHUNKS, lambda k: hand_4(k, p < 4, p > 3))

    def from_y(which, buf, d):
        o = (y + d) % 4
        copy(buf.at[o], buf.at[o], y_s.at[which, 4 - d], y_r.at[which, 4 - d], far).wait_recv()

    loop(1, 4, lambda d: from_y(0, wy, d))
    wz[z] = jnp.sum(wy[...], axis=0)
    loop(1, n_z, lambda d: copy(wz.at[z], wz.at[z], z_s.at[0, d], z_r.at[0, d], at(p, z + d)).start())

    def from_z(which, buf, d):
        o = (z + d) % n_z
        copy(buf.at[o], buf.at[o], z_s.at[which, n_z - d], z_r.at[which, n_z - d], far).wait_recv()

    def wait_block(slot):
        loop(0, CHUNKS, lambda k: arrived(slot, k))

    def early_text(k):
        pl.when(k % 2 == 1)(lambda: wait_block(k))
        tile(0, k)

    def early_image(k):
        pl.when(k % 2 == 1)(lambda: wait_block(k + 5))
        tile(1, k)

    n_text = jnp.minimum(REACH, 7 - p) + 1
    n_image = jnp.minimum(REACH, p) + 1
    loop(0, n_text, early_text)
    loop(0, n_image, early_image)
    dl = jnp.sum(jnp.sum(diag[0] * logits[0, 0], axis=0, keepdims=True), axis=1, keepdims=True)

    side_x = 1 - half
    early_out[0:1] = as_row(lse_of(side_x))
    early_out[1:2] = jnp.log(weight)
    copy(early_out, early_z, ez_s, ez_r, far).start()
    copy(early_out, early_z, ez_s, ez_r, far).wait_recv()
    loop(0, 4, lambda j: copy(early_z, early.at[q], ef_s.at[j], ef_r.at[q], at(4 * (1 - half) + j, z)).start())

    loop(1, n_z, lambda d: from_z(0, wz, d))
    total_weight = jnp.sum(wz[...], axis=0)

    def hand_x(k):
        arrived(X_SLOT, k)
        pl.when(p < 2)(lambda: chunk_copy(X_SLOT, 2, k, at(p - 2, z), K_XT).start())
        pl.when(p > 5)(lambda: chunk_copy(X_SLOT, 7, k, at(p + 2, z), K_XI).start())
        pl.when((p >= 2) & (p < 4))(lambda: chunk_copy(X_SLOT, RELAY, k, at(p + 2, z), K_HX).start())
        pl.when((p >= 4) & (p < 6))(lambda: chunk_copy(X_SLOT, RELAY, k, at(p - 2, z), K_HX).start())

    def hand_relay(k):
        @pl.when((p >= 2) & (p < 6))
        def _():
            arrived(RELAY, k)
            pl.when(p >= 4)(lambda: chunk_copy(RELAY, 4, k, at(p + 2, z), K_HR).start())
            pl.when(p < 4)(lambda: chunk_copy(RELAY, 9, k, at(p - 2, z), K_HR).start())

    def late(k):
        pl.when(k < CHUNKS)(lambda: hand_x(k))

        @pl.when((k >= 1) & (k <= CHUNKS))
        def _():
            hand_relay(k - 1)
            hand_2(k - 1, p >= 6, p <= 1)

        pl.when(k >= 2)(lambda: hand_4(k - 2, p >= 4, p <= 3))

    loop(0, CHUNKS + 2, late)

    def late_tile(side, k, t):
        pl.when(k % 2 == 1)(lambda: wait_block(k + 5 * side))
        tile(side, k)
        v = logits[side, k]
        top = jnp.max(v, axis=0, keepdims=True)
        rp[q, pl.ds(t, 1)] = top + jnp.log(jnp.sum(jnp.exp(v - top), axis=0, keepdims=True))

    loop(n_text, REACH + 1, lambda k: late_tile(0, k, p + k - 8))
    loop(n_image, REACH + 1, lambda k: late_tile(1, k, p - k + 4))

    def same_half(d):
        return 4 * half + (q + d) % 4

    loop(1, 4, lambda d: copy(rp.at[q], rp.at[q], rp_s.at[d], rp_r.at[d], at(same_half(d), z)).start())
    row_lse, col_lse = lse_of(0), lse_of(1)
    log_w = wcol[1]
    alpha, beta = row_lse - log_w, col_lse - log_w
    ls[p, 0:1] = as_row(alpha)
    ls[p, 1:2] = as_row(beta)

    def mean_of(side):
        return jnp.sum(stat[side, 2], axis=1, keepdims=True) / jnp.sum(stat[side, 1], axis=1, keepdims=True)

    ls[p, 2:3, 0:128] = jnp.sum(wc * (row_lse + col_lse), axis=0, keepdims=True) - dl
    ls[p, 2:3, 128:256] = jnp.sum(wc * (mean_of(0) + mean_of(1)), axis=0, keepdims=True) - dl
    loop(1, 8, lambda d: copy(ls.at[p], ls.at[p], ls_s.at[d], ls_r.at[d], at(p + d, z)).start())

    def from_ls(d):
        o = (p + d) % 8
        copy(ls.at[o], ls.at[o], ls_s.at[8 - d], ls_r.at[8 - d], far).wait_recv()

    def from_rp(d):
        o = (q + d) % 4
        copy(rp.at[o], rp.at[o], rp_s.at[4 - d], rp_r.at[4 - d], far).wait_recv()

    loop(1, 8, from_ls)
    ay[y] = jnp.sum(ls[:, 2:3, :], axis=0)
    loop(1, 4, lambda d: copy(ay.at[y], ay.at[y], y_s.at[1, d], y_r.at[1, d], at(p, z, y + d)).start())
    loop(1, 4, from_rp)
    loop(0, 4, lambda j: copy(early_z, early.at[j], ef_s.at[j], ef_r.at[j], far).wait_recv())

    def coef(side, k):
        here = (p + k < 8) if side == 0 else (p >= k)
        t = (p + k) % 8 if side == 0 else (p - k + 4) % 8
        t = jnp.where(here, 0, t)
        o = (p + k) % 8 if side == 0 else (p - k + 8) % 8
        parts = [rp[j, pl.ds(t, 1)] for j in range(4)] + [early[t, 0:1]]
        top = functools.reduce(jnp.maximum, parts)
        merged = top + jnp.log(sum(jnp.exp(v - top) for v in parts)) - early[t, 1:2]
        theirs = jnp.where(here, ls[o, 1 - side:2 - side], merged)
        mine = alpha if side == 0 else beta
        v = logits[side, k]
        both = jnp.exp(v - theirs) + jnp.exp(v - jnp.concatenate([mine, mine], axis=1))
        if k == 0:
            both = both - diag[side]
        coefs[side, :, k * rows:(k + 1) * rows] = both.astype(jnp.bfloat16)

    for k in range(REACH + 1):
        coef(0, k)
        coef(1, k)

    loop(1, 4, lambda d: from_y(1, ay, d))
    az[z] = jnp.sum(ay[...], axis=0)
    loop(1, n_z, lambda d: copy(az.at[z], az.at[z], z_s.at[1, d], z_r.at[1, d], at(p, z + d)).start())

    n_pairs = 1.0 * rows * lax.axis_size("outer") * lax.axis_size("inner")
    gain = jnp.broadcast_to((temper * n_pairs) / (2.0 * total_weight[:, 0:1]), (1, blocks.shape[2]))
    for side, out in ((0, ig_ref), (1, tg_ref)):
        other = blocks[5 * side:5 * side + 5].reshape((REACH + 1) * rows, blocks.shape[2])
        acc = jnp.dot(coefs[side], other, preferred_element_type=F32)
        out[...] = (acc * gain).astype(out.dtype)

    def sent(k):
        def done(kind):
            chunk_copy(0, 0, k, far, kind).wait_send()

        for kind in (K_Z, K_XT, K_XI, K_C1, K_C2, K_C3, K_C4):
            done(kind)
        pl.when(p >= 2)(lambda: done(K_HT))
        pl.when(p <= 5)(lambda: done(K_HI))

        @pl.when((p >= 2) & (p < 6))
        def _():
            done(K_HX)
            done(K_HR)

    loop(0, CHUNKS, sent)
    loop(1, 8, lambda d: copy(wp.at[p], wp.at[p], p_s.at[d], p_r.at[d], far).wait_send())
    loop(1, 8, lambda d: copy(ls.at[p], ls.at[p], ls_s.at[d], ls_r.at[d], far).wait_send())
    loop(1, 4, lambda d: copy(rp.at[q], rp.at[q], rp_s.at[d], rp_r.at[d], far).wait_send())
    loop(0, 4, lambda j: copy(early_z, early.at[q], ef_s.at[j], ef_r.at[j], far).wait_send())
    copy(early_out, early_z, ez_s, ez_r, far).wait_send()
    for which, by, bz in ((0, wy, wz), (1, ay, az)):
        loop(1, 4, lambda d: copy(by.at[y], by.at[y], y_s.at[which, d], y_r.at[which, d], far).wait_send())
        loop(1, n_z, lambda d: copy(bz.at[z], bz.at[z], z_s.at[which, d], z_r.at[which, d], far).wait_send())

    loop(1, n_z, lambda d: from_z(1, az, d))
    sums = jnp.sum(az[...], axis=0)
    loss_ref[0] = jnp.max(sums[:, 0:128] / (2.0 * total_weight))
    sg_ref[0] = jnp.max(sums[:, 128:256] / (2.0 * total_weight * temper))


def per_device(image_embed, text_embed, positive, row_weight, logit_scale):
    rows, width = image_embed.shape
    n_z = 16
    vmem = pl.BlockSpec(memory_space=pltpu.VMEM)
    smem = pl.BlockSpec(memory_space=pltpu.SMEM)
    hbm = pl.BlockSpec(memory_space=pl.ANY)
    dma = pltpu.SemaphoreType.DMA
    loss, scale_grad, image_grad, text_grad = (None,) * 4
    image_grad, text_grad, loss, scale_grad = pl.pallas_call(
        functools.partial(kernel, rows, n_z),
        out_shape=[
            jax.ShapeDtypeStruct((rows, width), jnp.bfloat16),
            jax.ShapeDtypeStruct((rows, width), jnp.bfloat16),
            jax.ShapeDtypeStruct((1,), F32),
            jax.ShapeDtypeStruct((1,), F32),
        ],
        in_specs=[hbm, hbm, vmem, vmem, smem],
        out_specs=[vmem, vmem, smem, smem],
        scratch_shapes=[
            pltpu.VMEM((12, rows, width), jnp.bfloat16),
            pltpu.VMEM((2, REACH + 1, rows, rows), F32),
            pltpu.VMEM((2, rows, (REACH + 1) * rows), jnp.bfloat16),
            pltpu.VMEM((2, 3, rows, 128), F32),
            pltpu.VMEM((2, rows, rows), F32),
            pltpu.VMEM((2, rows, 128), F32),
            pltpu.VMEM((8, 4, rows), F32),
            pltpu.VMEM((4, 4, rows), F32),
            pltpu.VMEM((2, rows), F32),
            pltpu.VMEM((2, rows), F32),
            pltpu.VMEM((4, 2, rows), F32),
            pltpu.VMEM((8, 1, 128), F32),
            pltpu.VMEM((4, 1, 128), F32),
            pltpu.VMEM((n_z, 1, 128), F32),
            pltpu.VMEM((4, 1, 256), F32),
            pltpu.VMEM((n_z, 1, 256), F32),
            dma((2,)),
            dma((11, CHUNKS)),
            dma((12, CHUNKS)),
            dma((8,)), dma((8,)),
            dma((4,)), dma((4,)),
            dma, dma,
            dma((4,)), dma((4,)),
            dma((8,)), dma((8,)),
            dma((2, 4)), dma((2, 4)),
            dma((2, n_z)), dma((2, n_z)),
        ],
        compiler_params=pltpu.CompilerParams(
            collective_id=0, has_side_effects=True, vmem_limit_bytes=48 * 2**20
        ),
        name="contrast",
    )(
        image_embed, text_embed, positive,
        row_weight.astype(F32).reshape(1, rows), logit_scale,
    )
    return loss, scale_grad, image_grad, text_grad


def solution(mesh):
    both = ("outer", "inner")
    in_specs = (P(both, None), P(both, None), P(both, None), P(both), P())
    out_specs = (P(), P(), P(both, None), P(both, None))
    return jax.shard_map(per_device, mesh=mesh, in_specs=in_specs, out_specs=out_specs, check_vma=False)
```

time: 610 us -> 108 us (0.18)
  blocking collectives: 268 us -> 0 us
  starting transfers between devices: 166 us -> 0 us
  waiting for transfers between devices: 150 us -> 0 us
  Pallas kernels: 0 us -> 98.4 us
  matrix products: 10.3 us -> 0 us
    psum x2 -> x0, blocking collectives: 268 us -> none  [the longest x1 141 us: per_device(): lax.psum((loss_part, scale_part), ('outer', 'inner'))]
    ppermute x20 -> x0, starting transfers between devices: 166 us -> none  [passed_along(): return lax.ppermute(block, axis, route)]
    ppermute x20 -> x0, waiting for transfers between devices: 150 us -> none  [passed_along(): return lax.ppermute(block, axis, route)]
    pallas_call x0 -> x1, Pallas kernels: none -> 98.4 us  [per_device(): pl.pallas_call(functools.partial(kernel, rows, n_z), out_shape=[jax.Shape...]
    dot_general x15 -> x0, matrix products: 10.3 us -> none  [the longest x5 4.17 us: per_device(): jnp.einsum('rc,rd->cd', coef_tile, image_embed, preferred_element_type=jn...]
  transfers between devices with their start and end apart: 20 -> 0, of which waited for: 13 -> 0; matrix products, arithmetic and copies ran while one was open for 1% -> 0% of each run, Pallas kernels for 0% -> 0%
where the time goes in v1:
time: 108 us; the launch traced here: 107 us
  Pallas kernels  98.4 us (91%)
  between operations  4.76 us (4%)
  local copies, waits for them, and re-layouts  4.16 us (4%)
    pallas_call x1, Pallas kernels, per_device(): pl.pallas_call(functools.partial(kernel, rows, n_z), out_shape=[jax.Shape...  98.4 us
    unnamed x10, local copies, waits for them, and re-layouts  4.16 us

profile of v1, /device:TPU:1, one launch (start us, length us, event | category | flops | bytes accessed | tf_op | source)
XLA Modules:
  0.0 107.3 jit_solution(10260109695375134013)
XLA Ops:
  0.6 0.0 copy-start.3
  1.3 0.0 copy-done.3
  1.3 0.0 copy-start.2
  1.3 0.7 copy-done.2
  2.0 0.0 copy-start
  2.0 1.0 copy-done
  3.0 0.0 copy-start.1
  3.0 1.0 copy-done.1
  4.0 98.4 %contrast.1 = (bf16[256,768]{1,0:T(8,128)(2,1)S(1)}, bf16[256,768]{1,0:T(8,128)(2,1)S(1)}, f32[1]{0:T(128)}, f32[1]{0:T(128)}) custom-call(bf16[256,768]{1,0:T(8,128)(2,1)S(1)} %copy-done, bf16[256,768]{1,0:T(8,128)(2,1)S(1)} %copy-done.1, s32[1,256]{1,0:T(1,128)S(1)} %copy-done.2, f32[1,256]{1,0:T(1,128)S(1)} %bitcast.1, f32[1]{0:T(128)S(6)} %copy.13.scale_ref), custom_call_target="tpu_custom_call" | custom-call | tf_op jit(solution)/shard_map/contrast/pallas_call | solution.py:349
  103.6 0.7 copy.16
  104.3 0.7 copy.17
  (1 shorter events, 0.0 us)
Async XLA Ops:
  0.6 0.7 copy-start.3
  1.3 0.7 copy-start.2
  2.0 1.0 copy-start
  3.0 1.0 copy-start.1

commit v2 on v1

v2 whole, which is shorter than its diff:
```python
import functools

import jax
import jax.numpy as jnp
from jax import lax
from jax.experimental import pallas as pl
from jax.experimental.pallas import tpu as pltpu
from jax.sharding import PartitionSpec as P

MESH = pl.DeviceIdType.MESH
CHUNKS = 4
LAG = 1
REACH = 4
RELAY = 10
(K_Z, K_XT, K_XI, K_HT, K_HI, K_HR, K_C1, K_C2, K_C3, K_C4) = range(10)
LOW = -1e30
F32 = jnp.float32


def loop(low, high, body):
    def step(k, carry):
        body(k)
        return carry

    lax.fori_loop(low, high, step, 0)


def dot_nt(a, b):
    return lax.dot_general(a, b, (((1,), (1,)), ((), ())), preferred_element_type=F32)


def spread(row):
    return jnp.transpose(jnp.broadcast_to(row, (128, row.shape[1])))


def as_row(col):
    return jnp.transpose(col)[0:1]


def kernel(
    rows, n_z, img_ref, txt_ref, pos_hbm, w_hbm, scale_ref,
    ig_ref, tg_ref, loss_ref, sg_ref,
    blocks, logits, coefs, stat, diag, wcol, ls, rp, early_out, early_z, early, wp, wy, wz, ay, az,
    grads, pos_ref, w_ref, local_sem, send, recv, whole, ls_s, ls_r, rp_s, rp_r, ez_s, ez_r, ef_s, ef_r, p_s, p_r, y_s, y_r, z_s, z_r,
):
    part = rows // CHUNKS
    outer, inner = lax.axis_index("outer"), lax.axis_index("inner")
    z_low = n_z // 2
    y, z = outer // z_low, (inner // 8) * z_low + outer % z_low
    p = inner % 8
    even = p % 2 == 0
    mate = p + 1 - 2 * (p % 2)
    half = p // 4
    q = p % 4

    def at(p_, z_, y_=None):
        y_ = y if y_ is None else (y_ + 4) % 4
        z_ = (z_ + n_z) % n_z
        return (y_ * z_low + z_ % z_low, (z_ // z_low) * 8 + (p_ + 8) % 8)

    far = at(p, z + z_low)
    cross = at(6 - p + 2 * (p % 2), z + z_low)

    def far_first(j):
        return n_z // 2 + (j // 2) * (1 - 2 * (j % 2))

    def copy(src, dst, s_sem, r_sem, dev):
        return pltpu.make_async_remote_copy(
            src_ref=src, dst_ref=dst, send_sem=s_sem, recv_sem=r_sem, device_id=dev, device_id_type=MESH
        )

    barrier = pltpu.get_barrier_semaphore()

    def hello(dev):
        pl.semaphore_signal(barrier, inc=1, device_id=dev, device_id_type=MESH)

    hello(cross)
    loop(1, n_z, lambda j: hello(at(p, z + far_first(j))))
    loop(1, 4, lambda d: hello(at(p, z, y + d)))
    loop(1, 8, lambda d: hello(at(p + d, z)))
    text_in = pltpu.make_async_copy(txt_ref, blocks.at[0], local_sem.at[0])
    image_in = pltpu.make_async_copy(img_ref, blocks.at[5], local_sem.at[1])
    text_in.start()
    image_in.start()
    pos_in = pltpu.make_async_copy(pos_hbm, pos_ref, local_sem.at[2])
    w_in = pltpu.make_async_copy(w_hbm, w_ref, local_sem.at[3])
    pos_in.start()
    w_in.start()
    pl.semaphore_wait(barrier, 7 + 3 + n_z)
    text_in.wait()
    image_in.wait()
    pos_in.wait()
    w_in.wait()

    def chunk_copy(src, dst, k, dev, kind):
        r = pl.ds(pl.multiple_of(k * part, part), part)
        return copy(blocks.at[src, r], blocks.at[dst, r], send.at[kind], recv.at[dst, k], dev)

    def last_copy(src, dst, k, dev, kind):
        r = pl.ds(pl.multiple_of(k * part, part), part)
        return copy(blocks.at[src, r], blocks.at[dst, r], send.at[kind], whole.at[dst], dev)

    def arrived(slot, k):
        chunk_copy(slot, slot, k, far, 0).wait_recv()

    def all_arrived(slot):
        copy(blocks.at[slot], blocks.at[slot], send.at[0], whole.at[slot], far).wait_recv()

    crossing = jnp.where(half == 0, 0, 5)
    landing = jnp.where(p < 2, 2, jnp.where(p > 5, 7, RELAY))
    loop(0, CHUNKS, lambda k: chunk_copy(crossing, landing, k, cross, K_Z).start())

    def send_own(k):
        pl.when(p >= 2)(lambda: chunk_copy(0, 2, k, at(p - 2, z), K_XT).start())
        pl.when(p <= 5)(lambda: chunk_copy(5, 7, k, at(p + 2, z), K_XI).start())
        pl.when(even)(lambda: last_copy(5, 6, k, at(mate, z), K_C1).start())
        pl.when(~even)(lambda: last_copy(0, 1, k, at(mate, z), K_C1).start())

    loop(0, CHUNKS, send_own)

    weight = w_ref[...]
    wcol[0] = spread(weight)
    wcol[1] = spread(jnp.log(weight))
    wp[p] = jnp.broadcast_to(jnp.sum(weight, axis=1, keepdims=True), (1, 128))
    loop(1, 8, lambda d: copy(wp.at[p], wp.at[p], p_s, p_r, at(p + d, z)).start())

    place = pos_ref[...]
    lanes = lax.broadcasted_iota(jnp.int32, (rows, rows), 1)
    subs = lax.broadcasted_iota(jnp.int32, (rows, rows), 0)
    place_col = spread(place.astype(F32)).astype(jnp.int32)[:, 0:1]
    wc = wcol[0]
    w_sub = jnp.concatenate([wc, wc], axis=1)
    diag[0] = jnp.where(lanes == place_col, w_sub + weight, 0.0)
    diag[1] = jnp.where(subs == place, w_sub + weight, 0.0)
    stat[:, 0] = jnp.full((2, rows, 128), LOW, F32)
    stat[:, 1:3] = jnp.zeros((2, 2, rows, 128), F32)
    rp[q] = jnp.full((4, rows), LOW, F32)
    temper = scale_ref[0]

    def tile(side, k):
        own = jnp.where(side == 0, 5, 0)
        other = jnp.where(side == 0, 0, 5) + k
        t = temper * dot_nt(blocks[own], blocks[other])
        logits[side, k] = t
        old = stat[side, 0]
        new = jnp.maximum(old, jnp.max(t, axis=1, keepdims=True))
        keep = jnp.exp(old - new)
        t0, t1 = t[:, :128], t[:, 128:]
        e0, e1 = jnp.exp(t0 - new), jnp.exp(t1 - new)
        stat[side, 0] = new
        stat[side, 1] = stat[side, 1] * keep + (e0 + e1)
        stat[side, 2] = stat[side, 2] * keep + (e0 * t0 + e1 * t1)

    def lse_of(side):
        total = jnp.broadcast_to(jnp.sum(stat[side, 1], axis=1, keepdims=True), (rows, 128))
        return stat[side, 0] + jnp.log(total)

    def hand_2(k, text, image):
        @pl.when(text)
        def _():
            arrived(2, k)
            pl.when(p >= 2)(lambda: chunk_copy(2, 4, k, at(p - 2, z), K_HT).start())
            last_copy(2, jnp.where(even, 1, 3), k, at(mate, z), K_C2).start()

        @pl.when(image)
        def _():
            arrived(7, k)
            pl.when(p <= 5)(lambda: chunk_copy(7, 9, k, at(p + 2, z), K_HI).start())
            last_copy(7, jnp.where(even, 8, 6), k, at(mate, z), K_C4).start()

    def hand_4(k, text, image):
        @pl.when(text)
        def _():
            arrived(4, k)
            pl.when(even)(lambda: last_copy(4, 3, k, at(mate, z), K_C3).start())

        @pl.when(image)
        def _():
            arrived(9, k)
            pl.when(~even)(lambda: last_copy(9, 8, k, at(mate, z), K_C3).start())

    loop(0, CHUNKS, lambda k: hand_2(k, p < 6, p > 1))

    copy(wp.at[0:7], wp.at[0:7], p_s, p_r, far).wait_recv()
    wy[y] = jnp.sum(wp[...], axis=0)
    loop(1, 4, lambda d: copy(wy.at[y], wy.at[y], y_s.at[0], y_r.at[0], at(p, z, y + d)).start())

    loop(0, CHUNKS, lambda k: hand_4(k, p < 4, p > 3))

    def from_y(which, buf):
        copy(buf.at[0:3], buf.at[0:3], y_s.at[which], y_r.at[which], far).wait_recv()

    from_y(0, wy)
    wz[z] = jnp.sum(wy[...], axis=0)

    def to_z(which, buf, d):
        copy(buf.at[z], buf.at[z], z_s.at[which], z_r.at[which], at(p, z + d)).start()

    loop(1, n_z, lambda j: to_z(0, wz, far_first(j)))

    def from_z(which, buf):
        copy(buf.at[1:n_z], buf.at[1:n_z], z_s.at[which], z_r.at[which], far).wait_recv()

    def wait_block(slot):
        all_arrived(slot)

    def early_text(k):
        pl.when(k % 2 == 1)(lambda: wait_block(k))
        tile(0, k)

    def early_image(k):
        pl.when(k % 2 == 1)(lambda: wait_block(k + 5))
        tile(1, k)

    n_text = jnp.minimum(REACH, 7 - p) + 1
    n_image = jnp.minimum(REACH, p) + 1
    loop(0, n_text, early_text)
    loop(0, n_image, early_image)
    dl = jnp.sum(jnp.sum(diag[0] * logits[0, 0], axis=0, keepdims=True), axis=1, keepdims=True)

    side_x = 1 - half
    early_out[0:1] = as_row(lse_of(side_x))
    early_out[1:2] = jnp.log(weight)
    copy(early_out, early_z, ez_s, ez_r, far).start()

    def hand_relay(k):
        @pl.when((p >= 2) & (p < 6))
        def _():
            arrived(RELAY, k)
            pl.when(p >= 4)(lambda: chunk_copy(RELAY, 4, k, at(p + 2, z), K_HR).start())
            pl.when(p < 4)(lambda: chunk_copy(RELAY, 9, k, at(p - 2, z), K_HR).start())

    def late(k):
        @pl.when(k < CHUNKS)
        def _():
            hand_relay(k)
            hand_2(k, p >= 6, p <= 1)

        pl.when(k >= LAG)(lambda: hand_4(k - LAG, p >= 4, p <= 3))

    loop(0, CHUNKS + LAG, late)
    copy(early_out, early_z, ez_s, ez_r, far).wait_recv()
    loop(0, 4, lambda j: copy(early_z, early.at[q], ef_s, ef_r, at(4 * (1 - half) + j, z)).start())

    def late_tile(side, k, t):
        pl.when(k % 2 == 1)(lambda: wait_block(k + 5 * side))
        tile(side, k)
        v = logits[side, k]
        top = jnp.max(v, axis=0, keepdims=True)
        rp[q, pl.ds(t, 1)] = top + jnp.log(jnp.sum(jnp.exp(v - top), axis=0, keepdims=True))

    loop(n_text, REACH + 1, lambda k: late_tile(0, k, p + k - 8))
    loop(n_image, REACH + 1, lambda k: late_tile(1, k, p - k + 4))

    def same_half(d):
        return 4 * half + (q + d) % 4

    loop(1, 4, lambda d: copy(rp.at[q], rp.at[q], rp_s, rp_r, at(same_half(d), z)).start())
    row_lse, col_lse = lse_of(0), lse_of(1)
    log_w = wcol[1]
    alpha, beta = row_lse - log_w, col_lse - log_w
    ls[p, 0:1] = as_row(alpha)
    ls[p, 1:2] = as_row(beta)

    def mean_of(side):
        return jnp.sum(stat[side, 2], axis=1, keepdims=True) / jnp.sum(stat[side, 1], axis=1, keepdims=True)

    ls[p, 2:3, 0:128] = jnp.sum(wc * (row_lse + col_lse), axis=0, keepdims=True) - dl
    ls[p, 2:3, 128:256] = jnp.sum(wc * (mean_of(0) + mean_of(1)), axis=0, keepdims=True) - dl
    loop(1, 8, lambda d: copy(ls.at[p], ls.at[p], ls_s, ls_r, at(p + d, z)).start())

    from_z(0, wz)
    total_weight = jnp.sum(wz[...], axis=0)
    n_pairs = 1.0 * rows * lax.axis_size("outer") * lax.axis_size("inner")
    factor = n_pairs / (2.0 * total_weight)
    log_f = jnp.log(factor)
    log_f2 = jnp.concatenate([log_f, log_f], axis=1)

    copy(ls.at[0:7], ls.at[0:7], ls_s, ls_r, far).wait_recv()
    ay[y] = jnp.sum(ls[:, 2:3, :], axis=0)
    loop(1, 4, lambda d: copy(ay.at[y], ay.at[y], y_s.at[1], y_r.at[1], at(p, z, y + d)).start())
    copy(rp.at[0:3], rp.at[0:3], rp_s, rp_r, far).wait_recv()
    copy(early, early, ef_s, ef_r, far).wait_recv()

    def coef(side, k):
        here = (p + k < 8) if side == 0 else (p >= k)
        t = (p + k) % 8 if side == 0 else (p - k + 4) % 8
        t = jnp.where(here, 0, t)
        o = (p + k) % 8 if side == 0 else (p - k + 8) % 8
        parts = [rp[j, pl.ds(t, 1)] for j in range(4)] + [early[t, 0:1]]
        top = functools.reduce(jnp.maximum, parts)
        merged = top + jnp.log(sum(jnp.exp(v - top) for v in parts)) - early[t, 1:2]
        theirs = jnp.where(here, ls[o, 1 - side:2 - side], merged)
        mine = (alpha if side == 0 else beta) - log_f
        theirs = theirs - log_f2
        v = logits[side, k]
        both = jnp.exp(v - theirs) + jnp.exp(v - jnp.concatenate([mine, mine], axis=1))
        if k == 0:
            both = both - diag[side] * factor[:, 0:1]
        coefs[side, :, k * rows:(k + 1) * rows] = both.astype(jnp.bfloat16)

    coef(0, 0)
    coef(1, 0)
    from_y(1, ay)
    az[z] = jnp.sum(ay[...], axis=0)
    loop(1, n_z, lambda j: to_z(1, az, far_first(j)))
    for k in range(1, REACH + 1):
        coef(0, k)
        coef(1, k)

    for side, out in ((0, ig_ref), (1, tg_ref)):
        other = blocks[5 * side:5 * side + 5].reshape((REACH + 1) * rows, blocks.shape[2])
        acc = jnp.dot(coefs[side], other, preferred_element_type=F32)
        grads[side] = (acc * temper).astype(out.dtype)
        pltpu.make_async_copy(grads.at[side], out, local_sem.at[side]).start()

    def sent(kind):
        copy(blocks.at[0], blocks.at[0], send.at[kind], whole.at[0], far).wait_send()

    for kind in (K_Z, K_C1, K_C2, K_C3, K_C4):
        sent(kind)

    @pl.when(p >= 2)
    def _():
        sent(K_XT)
        sent(K_HT)

    @pl.when(p <= 5)
    def _():
        sent(K_XI)
        sent(K_HI)

    pl.when((p >= 2) & (p < 6))(lambda: sent(K_HR))
    copy(wp.at[0:7], wp.at[0:7], p_s, p_r, far).wait_send()
    copy(ls.at[0:7], ls.at[0:7], ls_s, ls_r, far).wait_send()
    copy(rp.at[0:3], rp.at[0:3], rp_s, rp_r, far).wait_send()
    copy(early, early, ef_s, ef_r, far).wait_send()
    copy(early_out, early_z, ez_s, ez_r, far).wait_send()
    for which, by, bz in ((0, wy, wz), (1, ay, az)):
        copy(by.at[0:3], by.at[0:3], y_s.at[which], y_r.at[which], far).wait_send()
        copy(bz.at[1:n_z], bz.at[1:n_z], z_s.at[which], z_r.at[which], far).wait_send()

    from_z(1, az)
    sums = jnp.sum(az[...], axis=0)
    loss_ref[0] = jnp.max(sums[:, 0:128] / (2.0 * total_weight))
    for side, out in ((0, ig_ref), (1, tg_ref)):
        pltpu.make_async_copy(grads.at[side], out, local_sem.at[side]).wait()
    sg_ref[0] = jnp.max(sums[:, 128:256] / (2.0 * total_weight * temper))


def per_device(image_embed, text_embed, positive, row_weight, logit_scale):
    rows, width = image_embed.shape
    n_z = 16
    smem = pl.BlockSpec(memory_space=pltpu.SMEM)
    hbm = pl.BlockSpec(memory_space=pltpu.HBM)
    dma = pltpu.SemaphoreType.DMA
    image_grad, text_grad, loss, scale_grad = pl.pallas_call(
        functools.partial(kernel, rows, n_z),
        out_shape=[
            jax.ShapeDtypeStruct((rows, width), jnp.bfloat16),
            jax.ShapeDtypeStruct((rows, width), jnp.bfloat16),
            jax.ShapeDtypeStruct((1,), F32),
            jax.ShapeDtypeStruct((1,), F32),
        ],
        in_specs=[hbm, hbm, hbm, hbm, smem],
        out_specs=[hbm, hbm, smem, smem],
        scratch_shapes=[
            pltpu.VMEM((11, rows, width), jnp.bfloat16),
            pltpu.VMEM((2, REACH + 1, rows, rows), F32),
            pltpu.VMEM((2, rows, (REACH + 1) * rows), jnp.bfloat16),
            pltpu.VMEM((2, 3, rows, 128), F32),
            pltpu.VMEM((2, rows, rows), F32),
            pltpu.VMEM((2, rows, 128), F32),
            pltpu.VMEM((8, 4, rows), F32),
            pltpu.VMEM((4, 4, rows), F32),
            pltpu.VMEM((2, rows), F32),
            pltpu.VMEM((2, rows), F32),
            pltpu.VMEM((4, 2, rows), F32),
            pltpu.VMEM((8, 1, 128), F32),
            pltpu.VMEM((4, 1, 128), F32),
            pltpu.VMEM((n_z, 1, 128), F32),
            pltpu.VMEM((4, 1, 256), F32),
            pltpu.VMEM((n_z, 1, 256), F32),
            pltpu.VMEM((2, rows, width), jnp.bfloat16),
            pltpu.VMEM((1, rows), jnp.int32),
            pltpu.VMEM((1, rows), F32),
            dma((4,)),
            dma((10,)),
            dma((11, CHUNKS)),
            dma((9,)),
            dma, dma,
            dma, dma,
            dma, dma,
            dma, dma,
            dma, dma,
            dma((2,)), dma((2,)),
            dma((2,)), dma((2,)),
        ],
        compiler_params=pltpu.CompilerParams(
            collective_id=0, has_side_effects=True, vmem_limit_bytes=62 * 2**20
        ),
        name="contrast",
    )(
        image_embed, text_embed, positive,
        row_weight.astype(F32).reshape(1, rows), logit_scale,
    )
    return loss, scale_grad, image_grad, text_grad


def solution(mesh):
    both = ("outer", "inner")
    in_specs = (P(both, None), P(both, None), P(both, None), P(both), P())
    out_specs = (P(), P(), P(both, None), P(both, None))
    return jax.shard_map(per_device, mesh=mesh, in_specs=in_specs, out_specs=out_specs, check_vma=False)
```

time: 108 us -> 87.6 us (0.81)
  Pallas kernels: 98.4 us -> 79.5 us
  local copies, waits for them, and re-layouts: 4.16 us -> 2.57 us
    pallas_call x1, Pallas kernels: 98.4 us -> 79.5 us  [per_device(): pl.pallas_call(functools.partial(kernel, rows, n_z), out_shape=[jax.Shape...]
    unnamed x10 -> x6, local copies, waits for them, and re-layouts: 4.16 us -> 2.57 us
where the time goes in v2:
time: 87.6 us; the launch traced here: 87.4 us
  Pallas kernels  79.5 us (91%)
  between operations  4.84 us (6%)
  local copies, waits for them, and re-layouts  2.57 us (3%)
    pallas_call x1, Pallas kernels, per_device(): pl.pallas_call(functools.partial(kernel, rows, n_z), out_shape=[jax.Shape...  79.5 us
    unnamed x6, local copies, waits for them, and re-layouts  2.57 us

profile of v2, /device:TPU:1, one launch (start us, length us, event | category | flops | bytes accessed | tf_op | source)
XLA Modules:
  0.0 87.4 jit_solution(7420666366050708860)
XLA Ops:
  0.6 0.0 copy-start.1
  1.3 0.0 copy-done.1
  1.3 0.6 reshape.15
  1.9 79.5 %contrast.1 = (bf16[256,768]{1,0:T(8,128)(2,1)}, bf16[256,768]{1,0:T(8,128)(2,1)}, f32[1]{0:T(128)}, f32[1]{0:T(128)}) custom-call(bf16[256,768]{1,0:T(8,128)(2,1)} %img_ref.1, bf16[256,768]{1,0:T(8,128)(2,1)} %txt_ref.1, s32[1,256]{1,0:T(1,128)} %pos_hbm.1, f32[1,256]{1,0:T(1,128)} %bitcast.1, f32[1]{0:T(128)S(6)} %copy.13.scale_ref), custom_call_target="tpu_custom_call" | custom-call | tf_op jit(solution)/shard_map/contrast/pallas_call | solution.py:357
  82.6 0.0 copy-start
  82.6 1.8 %copy.16 = bf16[256,768]{1,0:T(8,128)(2,1)} copy(bf16[256,768]{1,0:T(8,128)(2,1)} %get-tuple-element.18) | data formatting | bytes 786432
  84.4 0.0 copy-done
  84.4 0.7 copy.17
Async XLA Ops:
  0.6 0.7 copy-start.1
  82.6 1.8 %copy-start = (bf16[256,768]{1,0:T(8,128)(2,1)S(1)}, bf16[256,768]{1,0:T(8,128)(2,1)}, u32[]{:S(2)}) copy-start(bf16[256,768]{1,0:T(8,128)(2,1)} %get-tuple-element.19) | copy-start | bytes 1179652

commit v3 on v2

--- a/solution.py
+++ b/solution.py
@@ -8,11 +8,13 @@
 from jax.sharding import PartitionSpec as P
 
 MESH = pl.DeviceIdType.MESH
-CHUNKS = 4
-LAG = 1
+CHUNKS = 8
+DUAL = 2
+LAG = 2
 REACH = 4
 RELAY = 10
-(K_Z, K_XT, K_XI, K_HT, K_HI, K_HR, K_C1, K_C2, K_C3, K_C4) = range(10)
+HANDED_ON = (2, 4, 7, 9, RELAY)
+(K_Z, K_XT, K_XI, K_HT, K_HI, K_HR, K_C1, K_C2, K_C3, K_C4, K_D, K_DR) = range(12)
 LOW = -1e30
 F32 = jnp.float32
 
@@ -40,8 +42,8 @@
 def kernel(
     rows, n_z, img_ref, txt_ref, pos_hbm, w_hbm, scale_ref,
     ig_ref, tg_ref, loss_ref, sg_ref,
-    blocks, logits, coefs, stat, diag, wcol, ls, rp, early_out, early_z, early, wp, wy, wz, ay, az,
-    grads, pos_ref, w_ref, local_sem, send, recv, whole, ls_s, ls_r, rp_s, rp_r, ez_s, ez_r, ef_s, ef_r, p_s, p_r, y_s, y_r, z_s, z_r,
+    blocks, logits, coefs, stat, diag, wcol, ls, rp, early_out, early_z, early, wy, wz, ay, az,
+    grads, pos_ref, w_ref, local_sem, send, recv, whole, ls_s, ls_r, rp_s, rp_r, ez_s, ez_r, ef_s, ef_r, y_s, y_r, z_s, z_r,
 ):
     part = rows // CHUNKS
     outer, inner = lax.axis_index("outer"), lax.axis_index("inner")
@@ -54,15 +56,22 @@
     q = p % 4
 
     def at(p_, z_, y_=None):
-        y_ = y if y_ is None else (y_ + 4) % 4
-        z_ = (z_ + n_z) % n_z
-        return (y_ * z_low + z_ % z_low, (z_ // z_low) * 8 + (p_ + 8) % 8)
+        y_ = y if y_ is None else lax.rem(y_, 4)
+        if z_ is not z:
+            z_ = lax.rem(z_ + n_z, n_z)
+        return (y_ * z_low + lax.rem(z_, z_low), lax.div(z_, z_low) * 8 + lax.rem(p_ + 8, 8))
 
     far = at(p, z + z_low)
+    other_core, left, right = at(mate, z), at(p - 2, z), at(p + 2, z)
     cross = at(6 - p + 2 * (p % 2), z + z_low)
 
+    here = y * 8 + p
+
+    def near(e):
+        return at(p + lax.rem(e, 8), z, y + lax.div(e, 8))
+
     def far_first(j):
-        return n_z // 2 + (j // 2) * (1 - 2 * (j % 2))
+        return n_z // 2 + lax.div(j, 2) * (1 - 2 * lax.rem(j, 2))
 
     def copy(src, dst, s_sem, r_sem, dev):
         return pltpu.make_async_remote_copy(
@@ -76,8 +85,7 @@
 
     hello(cross)
     loop(1, n_z, lambda j: hello(at(p, z + far_first(j))))
-    loop(1, 4, lambda d: hello(at(p, z, y + d)))
-    loop(1, 8, lambda d: hello(at(p + d, z)))
+    loop(1, 32, lambda e: hello(near(e)))
     text_in = pltpu.make_async_copy(txt_ref, blocks.at[0], local_sem.at[0])
     image_in = pltpu.make_async_copy(img_ref, blocks.at[5], local_sem.at[1])
     text_in.start()
@@ -86,15 +94,16 @@
     w_in = pltpu.make_async_copy(w_hbm, w_ref, local_sem.at[3])
     pos_in.start()
     w_in.start()
-    pl.semaphore_wait(barrier, 7 + 3 + n_z)
+    pl.semaphore_wait(barrier, 31 + n_z)
     text_in.wait()
     image_in.wait()
     pos_in.wait()
     w_in.wait()
 
-    def chunk_copy(src, dst, k, dev, kind):
+    def chunk_copy(src, dst, k, dev, kind, row=None):
         r = pl.ds(pl.multiple_of(k * part, part), part)
-        return copy(blocks.at[src, r], blocks.at[dst, r], send.at[kind], recv.at[dst, k], dev)
+        row = HANDED_ON.index(dst) if row is None else row
+        return copy(blocks.at[src, r], blocks.at[dst, r], send.at[kind], recv.at[row, k], dev)
 
     def last_copy(src, dst, k, dev, kind):
         r = pl.ds(pl.multiple_of(k * part, part), part)
@@ -108,21 +117,22 @@
 
     crossing = jnp.where(half == 0, 0, 5)
     landing = jnp.where(p < 2, 2, jnp.where(p > 5, 7, RELAY))
-    loop(0, CHUNKS, lambda k: chunk_copy(crossing, landing, k, cross, K_Z).start())
+    landing_row = jnp.where(p < 2, 0, jnp.where(p > 5, 2, 4))
+    loop(0, CHUNKS, lambda k: chunk_copy(crossing, landing, k, cross, K_Z, landing_row).start())
 
     def send_own(k):
-        pl.when(p >= 2)(lambda: chunk_copy(0, 2, k, at(p - 2, z), K_XT).start())
-        pl.when(p <= 5)(lambda: chunk_copy(5, 7, k, at(p + 2, z), K_XI).start())
-        pl.when(even)(lambda: last_copy(5, 6, k, at(mate, z), K_C1).start())
-        pl.when(~even)(lambda: last_copy(0, 1, k, at(mate, z), K_C1).start())
+        pl.when(p >= 2)(lambda: chunk_copy(0, 2, k, left, K_XT).start())
+        pl.when(p <= 5)(lambda: chunk_copy(5, 7, k, right, K_XI).start())
+        pl.when(even)(lambda: last_copy(5, 6, k, other_core, K_C1).start())
+        pl.when(~even)(lambda: last_copy(0, 1, k, other_core, K_C1).start())
 
     loop(0, CHUNKS, send_own)
 
-    weight = w_ref[...]
+    weight = w_ref[...].astype(F32).reshape(1, rows)
     wcol[0] = spread(weight)
     wcol[1] = spread(jnp.log(weight))
-    wp[p] = jnp.broadcast_to(jnp.sum(weight, axis=1, keepdims=True), (1, 128))
-    loop(1, 8, lambda d: copy(wp.at[p], wp.at[p], p_s, p_r, at(p + d, z)).start())
+    wy[here] = jnp.broadcast_to(jnp.sum(weight, axis=1, keepdims=True), (1, 128))
+    loop(1, 32, lambda e: copy(wy.at[here], wy.at[here], y_s.at[0], y_r.at[0], near(e)).start())
 
     place = pos_ref[...]
     lanes = lax.broadcasted_iota(jnp.int32, (rows, rows), 1)
@@ -159,36 +169,42 @@
         @pl.when(text)
         def _():
             arrived(2, k)
-            pl.when(p >= 2)(lambda: chunk_copy(2, 4, k, at(p - 2, z), K_HT).start())
-            last_copy(2, jnp.where(even, 1, 3), k, at(mate, z), K_C2).start()
+
+            @pl.when(p >= 2)
+            def _():
+                chunk_copy(2, 4, k, left, K_HT).start()
+                pl.when(even & (k >= CHUNKS - DUAL))(lambda: last_copy(2, 3, k, at(p - 1, z), K_D).start())
+
+            last_copy(2, jnp.where(even, 1, 3), k, other_core, K_C2).start()
 
         @pl.when(image)
         def _():
             arrived(7, k)
-            pl.when(p <= 5)(lambda: chunk_copy(7, 9, k, at(p + 2, z), K_HI).start())
-            last_copy(7, jnp.where(even, 8, 6), k, at(mate, z), K_C4).start()
+
+            @pl.when(p <= 5)
+            def _():
+                chunk_copy(7, 9, k, right, K_HI).start()
+                pl.when(~even & (k >= CHUNKS - DUAL))(lambda: last_copy(7, 8, k, at(p + 1, z), K_D).start())
+
+            last_copy(7, jnp.where(even, 8, 6), k, other_core, K_C4).start()
 
     def hand_4(k, text, image):
         @pl.when(text)
         def _():
             arrived(4, k)
-            pl.when(even)(lambda: last_copy(4, 3, k, at(mate, z), K_C3).start())
+            pl.when(even & (k < CHUNKS - DUAL))(lambda: last_copy(4, 3, k, other_core, K_C3).start())
 
         @pl.when(image)
         def _():
             arrived(9, k)
-            pl.when(~even)(lambda: last_copy(9, 8, k, at(mate, z), K_C3).start())
+            pl.when(~even & (k < CHUNKS - DUAL))(lambda: last_copy(9, 8, k, other_core, K_C3).start())
 
     loop(0, CHUNKS, lambda k: hand_2(k, p < 6, p > 1))
 
-    copy(wp.at[0:7], wp.at[0:7], p_s, p_r, far).wait_recv()
-    wy[y] = jnp.sum(wp[...], axis=0)
-    loop(1, 4, lambda d: copy(wy.at[y], wy.at[y], y_s.at[0], y_r.at[0], at(p, z, y + d)).start())
-
     loop(0, CHUNKS, lambda k: hand_4(k, p < 4, p > 3))
 
     def from_y(which, buf):
-        copy(buf.at[0:3], buf.at[0:3], y_s.at[which], y_r.at[which], far).wait_recv()
+        copy(buf.at[1:32], buf.at[1:32], y_s.at[which], y_r.at[which], far).wait_recv()
 
     from_y(0, wy)
     wz[z] = jnp.sum(wy[...], axis=0)
@@ -227,8 +243,16 @@
         @pl.when((p >= 2) & (p < 6))
         def _():
             arrived(RELAY, k)
-            pl.when(p >= 4)(lambda: chunk_copy(RELAY, 4, k, at(p + 2, z), K_HR).start())
-            pl.when(p < 4)(lambda: chunk_copy(RELAY, 9, k, at(p - 2, z), K_HR).start())
+
+            @pl.when(p >= 4)
+            def _():
+                chunk_copy(RELAY, 4, k, right, K_HR).start()
+                pl.when(even & (k >= CHUNKS - DUAL))(lambda: last_copy(RELAY, 3, k, at(p + 3, z), K_DR).start())
+
+            @pl.when(p < 4)
+            def _():
+                chunk_copy(RELAY, 9, k, left, K_HR).start()
+                pl.when(~even & (k >= CHUNKS - DUAL))(lambda: last_copy(RELAY, 8, k, at(p - 3, z), K_DR).start())
 
     def late(k):
         @pl.when(k < CHUNKS)
@@ -237,10 +261,6 @@
             hand_2(k, p >= 6, p <= 1)
 
         pl.when(k >= LAG)(lambda: hand_4(k - LAG, p >= 4, p <= 3))
-
-    loop(0, CHUNKS + LAG, late)
-    copy(early_out, early_z, ez_s, ez_r, far).wait_recv()
-    loop(0, 4, lambda j: copy(early_z, early.at[q], ef_s, ef_r, at(4 * (1 - half) + j, z)).start())
 
     def late_tile(side, k, t):
         pl.when(k % 2 == 1)(lambda: wait_block(k + 5 * side))
@@ -249,38 +269,33 @@
         top = jnp.max(v, axis=0, keepdims=True)
         rp[q, pl.ds(t, 1)] = top + jnp.log(jnp.sum(jnp.exp(v - top), axis=0, keepdims=True))
 
-    loop(n_text, REACH + 1, lambda k: late_tile(0, k, p + k - 8))
-    loop(n_image, REACH + 1, lambda k: late_tile(1, k, p - k + 4))
+    def late_pair(j):
+        k = 2 - j % 2 + 2 * (j // 2)
+        pl.when(k >= n_text)(lambda: late_tile(0, k, p + k - 8))
+        pl.when(k >= n_image)(lambda: late_tile(1, k, p - k + 4))
+
+    loop(0, CHUNKS, late)
+    loop(0, 2, late_pair)
+    loop(CHUNKS, CHUNKS + LAG, late)
+    loop(2, 4, late_pair)
 
     def same_half(d):
         return 4 * half + (q + d) % 4
 
+    row_lse, col_lse = lse_of(0), lse_of(1)
+    def mean_of(side):
+        return jnp.sum(stat[side, 2], axis=1, keepdims=True) / jnp.sum(stat[side, 1], axis=1, keepdims=True)
+
+    ay[here, 0:1, 0:128] = jnp.sum(wc * (row_lse + col_lse), axis=0, keepdims=True) - dl
+    ay[here, 0:1, 128:256] = jnp.sum(wc * (mean_of(0) + mean_of(1)), axis=0, keepdims=True) - dl
+    loop(1, 32, lambda e: copy(ay.at[here], ay.at[here], y_s.at[1], y_r.at[1], near(e)).start())
     loop(1, 4, lambda d: copy(rp.at[q], rp.at[q], rp_s, rp_r, at(same_half(d), z)).start())
-    row_lse, col_lse = lse_of(0), lse_of(1)
     log_w = wcol[1]
     alpha, beta = row_lse - log_w, col_lse - log_w
     ls[p, 0:1] = as_row(alpha)
     ls[p, 1:2] = as_row(beta)
-
-    def mean_of(side):
-        return jnp.sum(stat[side, 2], axis=1, keepdims=True) / jnp.sum(stat[side, 1], axis=1, keepdims=True)
-
-    ls[p, 2:3, 0:128] = jnp.sum(wc * (row_lse + col_lse), axis=0, keepdims=True) - dl
-    ls[p, 2:3, 128:256] = jnp.sum(wc * (mean_of(0) + mean_of(1)), axis=0, keepdims=True) - dl
     loop(1, 8, lambda d: copy(ls.at[p], ls.at[p], ls_s, ls_r, at(p + d, z)).start())
 
-    from_z(0, wz)
-    total_weight = jnp.sum(wz[...], axis=0)
-    n_pairs = 1.0 * rows * lax.axis_size("outer") * lax.axis_size("inner")
-    factor = n_pairs / (2.0 * total_weight)
-    log_f = jnp.log(factor)
-    log_f2 = jnp.concatenate([log_f, log_f], axis=1)
-
-    copy(ls.at[0:7], ls.at[0:7], ls_s, ls_r, far).wait_recv()
-    ay[y] = jnp.sum(ls[:, 2:3, :], axis=0)
-    loop(1, 4, lambda d: copy(ay.at[y], ay.at[y], y_s.at[1], y_r.at[1], at(p, z, y + d)).start())
-    copy(rp.at[0:3], rp.at[0:3], rp_s, rp_r, far).wait_recv()
-    copy(early, early, ef_s, ef_r, far).wait_recv()
 
     def coef(side, k):
         here = (p + k < 8) if side == 0 else (p >= k)
@@ -299,12 +314,21 @@
             both = both - diag[side] * factor[:, 0:1]
         coefs[side, :, k * rows:(k + 1) * rows] = both.astype(jnp.bfloat16)
 
-    coef(0, 0)
-    coef(1, 0)
     from_y(1, ay)
     az[z] = jnp.sum(ay[...], axis=0)
     loop(1, n_z, lambda j: to_z(1, az, far_first(j)))
-    for k in range(1, REACH + 1):
+    copy(early_out, early_z, ez_s, ez_r, far).wait_recv()
+    loop(0, 4, lambda j: copy(early_z, early.at[q], ef_s, ef_r, at(4 * (1 - half) + j, z)).start())
+    copy(ls.at[0:7], ls.at[0:7], ls_s, ls_r, far).wait_recv()
+    copy(rp.at[0:3], rp.at[0:3], rp_s, rp_r, far).wait_recv()
+    from_z(0, wz)
+    total_weight = jnp.sum(wz[...], axis=0)
+    n_pairs = 1.0 * rows * lax.axis_size("outer") * lax.axis_size("inner")
+    factor = n_pairs / (2.0 * total_weight)
+    log_f = jnp.log(factor)
+    log_f2 = jnp.concatenate([log_f, log_f], axis=1)
+    copy(early, early, ef_s, ef_r, far).wait_recv()
+    for k in range(REACH + 1):
         coef(0, k)
         coef(1, k)
 
@@ -317,8 +341,16 @@
     def sent(kind):
         copy(blocks.at[0], blocks.at[0], send.at[kind], whole.at[0], far).wait_send()
 
-    for kind in (K_Z, K_C1, K_C2, K_C3, K_C4):
+    def sent_part(kind, chunks):
+        r = blocks.at[0, pl.ds(0, chunks * part)]
+        copy(r, r, send.at[kind], whole.at[0], far).wait_send()
+
+    for kind in (K_Z, K_C1, K_C2, K_C4):
         sent(kind)
+    sent_part(K_C3, CHUNKS - DUAL)
+    pl.when((p >= 2) & even)(lambda: sent_part(K_D, DUAL))
+    pl.when((p <= 5) & ~even)(lambda: sent_part(K_D, DUAL))
+    pl.when((p == 4) | (p == 3))(lambda: sent_part(K_DR, DUAL))
 
     @pl.when(p >= 2)
     def _():
@@ -331,13 +363,12 @@
         sent(K_HI)
 
     pl.when((p >= 2) & (p < 6))(lambda: sent(K_HR))
-    copy(wp.at[0:7], wp.at[0:7], p_s, p_r, far).wait_send()
     copy(ls.at[0:7], ls.at[0:7], ls_s, ls_r, far).wait_send()
     copy(rp.at[0:3], rp.at[0:3], rp_s, rp_r, far).wait_send()
     copy(early, early, ef_s, ef_r, far).wait_send()
     copy(early_out, early_z, ez_s, ez_r, far).wait_send()
     for which, by, bz in ((0, wy, wz), (1, ay, az)):
-        copy(by.at[0:3], by.at[0:3], y_s.at[which], y_r.at[which], far).wait_send()
+        copy(by.at[1:32], by.at[1:32], y_s.at[which], y_r.at[which], far).wait_send()
         copy(bz.at[1:n_z], bz.at[1:n_z], z_s.at[which], z_r.at[which], far).wait_send()
 
     from_z(1, az)
@@ -371,24 +402,22 @@
             pltpu.VMEM((2, 3, rows, 128), F32),
             pltpu.VMEM((2, rows, rows), F32),
             pltpu.VMEM((2, rows, 128), F32),
-            pltpu.VMEM((8, 4, rows), F32),
+            pltpu.VMEM((8, 2, rows), F32),
             pltpu.VMEM((4, 4, rows), F32),
             pltpu.VMEM((2, rows), F32),
             pltpu.VMEM((2, rows), F32),
             pltpu.VMEM((4, 2, rows), F32),
-            pltpu.VMEM((8, 1, 128), F32),
-            pltpu.VMEM((4, 1, 128), F32),
+            pltpu.VMEM((32, 1, 128), F32),
             pltpu.VMEM((n_z, 1, 128), F32),
-            pltpu.VMEM((4, 1, 256), F32),
+            pltpu.VMEM((32, 1, 256), F32),
             pltpu.VMEM((n_z, 1, 256), F32),
             pltpu.VMEM((2, rows, width), jnp.bfloat16),
             pltpu.VMEM((1, rows), jnp.int32),
-            pltpu.VMEM((1, rows), F32),
+            pltpu.VMEM((rows,), jnp.bfloat16),
             dma((4,)),
-            dma((10,)),
-            dma((11, CHUNKS)),
+            dma((12,)),
+            dma((len(HANDED_ON), CHUNKS)),
             dma((9,)),
-            dma, dma,
             dma, dma,
             dma, dma,
             dma, dma,
@@ -402,7 +431,7 @@
         name="contrast",
     )(
         image_embed, text_embed, positive,
-        row_weight.astype(F32).reshape(1, rows), logit_scale,
+        row_weight, logit_scale,
     )
     return loss, scale_grad, image_grad, text_grad
 

time: 87.6 us -> 84.2 us (0.961)
  Pallas kernels: 79.5 us -> 76.7 us
    pallas_call x1, Pallas kernels: 79.5 us -> 76.7 us  [per_device(): pl.pallas_call(functools.partial(kernel, rows, n_z), out_shape=[jax.Shape...]
    unnamed x6 -> x4, local copies, waits for them, and re-layouts: 2.57 us -> 2.57 us
where the time goes in v3:
time: 84.2 us; the launch traced here: 84 us
  Pallas kernels  76.7 us (91%)
  between operations  4.81 us (6%)
  local copies, waits for them, and re-layouts  2.57 us (3%)
    pallas_call x1, Pallas kernels, per_device(): pl.pallas_call(functools.partial(kernel, rows, n_z), out_shape=[jax.Shape...  76.7 us
    unnamed x4, local copies, waits for them, and re-layouts  2.57 us

profile of v3, /device:TPU:1, one launch (start us, length us, event | category | flops | bytes accessed | tf_op | source)
XLA Modules:
  0.0 84.0 jit_solution(1354604343897246087)
XLA Ops:
  1.3 76.7 %contrast.1 = (bf16[256,768]{1,0:T(8,128)(2,1)}, bf16[256,768]{1,0:T(8,128)(2,1)}, f32[1]{0:T(128)}, f32[1]{0:T(128)}) custom-call(bf16[256,768]{1,0:T(8,128)(2,1)} %img_ref.1, bf16[256,768]{1,0:T(8,128)(2,1)} %txt_ref.1, s32[1,256]{1,0:T(1,128)} %pos_hbm.1, bf16[256]{0:T(256)(128)(2,1)} %w_hbm.1, f32[1]{0:T(128)S(6)} %copy.13.scale_ref), custom_call_target="tpu_custom_call" | custom-call | tf_op jit(solution)/shard_map/contrast/pallas_call | solution.py:388
  79.2 0.0 copy-start
  79.2 1.8 %copy.16 = bf16[256,768]{1,0:T(8,128)(2,1)} copy(bf16[256,768]{1,0:T(8,128)(2,1)} %get-tuple-element.18) | data formatting | bytes 786432
  81.0 0.0 copy-done
  81.0 0.7 copy.17
Async XLA Ops:
  79.2 1.8 %copy-start = (bf16[256,768]{1,0:T(8,128)(2,1)S(1)}, bf16[256,768]{1,0:T(8,128)(2,1)}, u32[]{:S(2)}) copy-start(bf16[256,768]{1,0:T(8,128)(2,1)} %get-tuple-element.19) | copy-start | bytes 1179652

commit v4 on v3

--- a/solution.py
+++ b/solution.py
@@ -68,7 +68,7 @@
     here = y * 8 + p
 
     def near(e):
-        return at(p + lax.rem(e, 8), z, y + lax.div(e, 8))
+        return at(p + e % 8, z, y + e // 8)
 
     def far_first(j):
         return n_z // 2 + lax.div(j, 2) * (1 - 2 * lax.rem(j, 2))
@@ -288,7 +288,8 @@
 
     ay[here, 0:1, 0:128] = jnp.sum(wc * (row_lse + col_lse), axis=0, keepdims=True) - dl
     ay[here, 0:1, 128:256] = jnp.sum(wc * (mean_of(0) + mean_of(1)), axis=0, keepdims=True) - dl
-    loop(1, 32, lambda e: copy(ay.at[here], ay.at[here], y_s.at[1], y_r.at[1], near(e)).start())
+    for e in range(1, 32):
+        copy(ay.at[here], ay.at[here], y_s.at[1], y_r.at[1], near(e)).start()
     loop(1, 4, lambda d: copy(rp.at[q], rp.at[q], rp_s, rp_r, at(same_half(d), z)).start())
     log_w = wcol[1]
     alpha, beta = row_lse - log_w, col_lse - log_w
@@ -316,7 +317,8 @@
 
     from_y(1, ay)
     az[z] = jnp.sum(ay[...], axis=0)
-    loop(1, n_z, lambda j: to_z(1, az, far_first(j)))
+    for j in range(1, n_z):
+        to_z(1, az, n_z // 2 + j // 2 * (1 - 2 * (j % 2)))
     copy(early_out, early_z, ez_s, ez_r, far).wait_recv()
     loop(0, 4, lambda j: copy(early_z, early.at[q], ef_s, ef_r, at(4 * (1 - half) + j, z)).start())
     copy(ls.at[0:7], ls.at[0:7], ls_s, ls_r, far).wait_recv()

time: 84.2 us -> 84 us (level)
  no operation moved by 1% of the time
where the time goes in v4:
time: 84 us; the launch traced here: 83.9 us
  Pallas kernels  76.5 us (91%)
  between operations  4.81 us (6%)
  local copies, waits for them, and re-layouts  2.57 us (3%)
    pallas_call x1, Pallas kernels, per_device(): pl.pallas_call(functools.partial(kernel, rows, n_z), out_shape=[jax.Shape...  76.5 us
    unnamed x4, local copies, waits for them, and re-layouts  2.57 us

profile of v4, /device:TPU:1, one launch (start us, length us, event | category | flops | bytes accessed | tf_op | source)
XLA Modules:
  0.0 83.9 jit_solution(9437667264288296946)
XLA Ops:
  1.3 76.5 %contrast.1 = (bf16[256,768]{1,0:T(8,128)(2,1)}, bf16[256,768]{1,0:T(8,128)(2,1)}, f32[1]{0:T(128)}, f32[1]{0:T(128)}) custom-call(bf16[256,768]{1,0:T(8,128)(2,1)} %img_ref.1, bf16[256,768]{1,0:T(8,128)(2,1)} %txt_ref.1, s32[1,256]{1,0:T(1,128)} %pos_hbm.1, bf16[256]{0:T(256)(128)(2,1)} %w_hbm.1, f32[1]{0:T(128)S(6)} %copy.13.scale_ref), custom_call_target="tpu_custom_call" | custom-call | tf_op jit(solution)/shard_map/contrast/pallas_call | solution.py:390
  79.0 0.0 copy-start
  79.0 1.8 %copy.16 = bf16[256,768]{1,0:T(8,128)(2,1)} copy(bf16[256,768]{1,0:T(8,128)(2,1)} %get-tuple-element.18) | data formatting | bytes 786432
  80.9 0.0 copy-done
  80.9 0.7 copy.17
Async XLA Ops:
  79.0 1.8 %copy-start = (bf16[256,768]{1,0:T(8,128)(2,1)S(1)}, bf16[256,768]{1,0:T(8,128)(2,1)}, u32[]{:S(2)}) copy-start(bf16[256,768]{1,0:T(8,128)(2,1)} %get-tuple-element.19) | copy-start | bytes 1179652
